TPU v7x, 32 devices: a whole 2x2x4 slice. The times are simulated.
32 devices in a mesh: row: 4 (over z), col: 8 (over y, x, core).
Axes of the slice: x: 2, y: 2, z: 4, core: 2. Of those that a mesh axis runs over, the one named last changes fastest.
Arguments:
- points: float32 [64, 4096], P(None, ('row', 'col')), may hold values from -6 to 6
- targets: float32 [4096], P(('row', 'col')), may hold values from -6 to 6
- probes: float32 [32, 4096], P(None, ('row', 'col')), may hold values from -6 to 6
- lengthscale: float32 [1], replicated, may hold values from 3.5 to 5
- outputscale: float32 [1], replicated, may hold values from 0.5 to 2
- noise: float32 [1], replicated, may hold values from 0.05 to 0.5
Outputs:
- solution: float32 [33, 4096], P(None, ('row', 'col'))
- residual: float32 [33, 4096], P(None, ('row', 'col'))
- direction: float32 [33, 4096], P(None, ('row', 'col'))
- length_products: float32 [32, 4096], P(None, ('row', 'col'))
- scale_products: float32 [32, 4096], P(None, ('row', 'col'))
All inputs are finite; a program needn't handle non-finite values.
Results may differ from a plain program's by a relative error of at most 0.0003.
Values sent between devices are 32-bit elements; how exact they have to be, the bound alone decides.
A program may use at most 64 MiB of HBM per device.

v0:
```python
import jax
import jax.numpy as jnp
from jax import lax
from jax.sharding import PartitionSpec as P


def make_fold(row_x, width, inv_two, n_rhs, n_probes):
    sq_rows = jnp.sum(row_x * row_x, axis=0)
    n_rows = row_x.shape[1]
    feats = row_x.shape[0]

    def accumulate(carry, pieces, start):
        col_x, col_rhs = pieces
        count = col_x.shape[1] // width
        xs = jnp.transpose(col_x.reshape(feats, count, width), (1, 0, 2))
        bs = jnp.transpose(col_rhs.reshape(n_rhs, count, width), (1, 0, 2))

        def step(totals, item):
            x_block, b_block = item
            sq_cols = jnp.sum(x_block * x_block, axis=0)
            dots = lax.dot_general(
                x_block,
                row_x,
                (((0,), (0,)), ((), ())),
                precision=lax.Precision.HIGHEST,
                preferred_element_type=jnp.float32,
            )
            dist = jnp.maximum(sq_cols[:, None] + sq_rows[None, :] - 2.0 * dots, 0.0)
            kern = jnp.exp(-dist * inv_two)
            eb_new = totals[0] + jnp.dot(
                b_block, kern, precision=lax.Precision.HIGHEST, preferred_element_type=jnp.float32
            )
            ed_new = totals[1] + jnp.dot(
                b_block[1:],
                kern * dist,
                precision=lax.Precision.HIGHEST,
                preferred_element_type=jnp.float32,
            )
            return ((eb_new, ed_new), None)

        result, unused = lax.scan(step, carry, (xs, bs))
        return result

    init = (jnp.zeros((n_rhs, n_rows), jnp.float32), jnp.zeros((n_probes, n_rows), jnp.float32))
    return (accumulate, init)


def shards(points, targets, probes, lengthscale, outputscale, noise):
    rhs = jnp.concatenate([targets[None, :], probes], 0)
    width = points.shape[1]
    n_rhs = rhs.shape[0]
    n_probes = probes.shape[0]
    inv_two = 0.5 / (lengthscale[0] * lengthscale[0])
    row_x = lax.all_gather(points, "col", axis=1, tiled=True)
    accumulate, init = make_fold(row_x, width, inv_two, n_rhs, n_probes)
    eb_part, ed_part = accumulate(
        init,
        (
            lax.all_gather(points, "row", axis=1, tiled=True),
            lax.all_gather(rhs, "row", axis=1, tiled=True),
        ),
        jnp.int32(0),
    )
    eb, ed = (
        lax.psum_scatter(eb_part, "col", scatter_dimension=1, tiled=True),
        lax.psum_scatter(ed_part, "col", scatter_dimension=1, tiled=True),
    )
    scale = outputscale[0]
    kb = scale * eb + noise[0] * rhs
    scale_products = eb[1:]
    length_products = scale / lengthscale[0] ** 3 * ed
    norm_old, curv = lax.psum(
        (jnp.sum(rhs * rhs, axis=1), jnp.sum(rhs * kb, axis=1)), ("row", "col")
    )
    alpha = norm_old / curv
    residual = rhs - alpha[:, None] * kb
    norm_new = lax.psum(jnp.sum(residual * residual, axis=1), ("row", "col"))
    solution = alpha[:, None] * rhs
    direction = residual + (norm_new / norm_old)[:, None] * rhs
    return (solution, residual, direction, length_products, scale_products)


def solution(mesh):
    placed = (P(None, ("row", "col")), P(("row", "col")), P(None, ("row", "col")), P(), P(), P())
    return jax.shard_map(
        shards,
        mesh=mesh,
        in_specs=placed,
        out_specs=(
            P(None, ("row", "col")),
            P(None, ("row", "col")),
            P(None, ("row", "col")),
            P(None, ("row", "col")),
            P(None, ("row", "col")),
        ),
        check_vma=False,
    )
```

profile of v0, /device:TPU:0, one launch (start us, length us, event | category | flops | bytes accessed | tf_op | source)
XLA Modules:
  0.0 213.5 jit_solution(7860792618601942791)
XLA Ops:
  7.2 0.0 copy-start.4
  7.2 0.0 reduce-scatter.5.cloned.1.call-start
  7.2 11.5 %all_gather.11 = f32[64,1024]{1,0:T(8,128)S(1)} all-gather(f32[64,128]{1,0:T(8,128)} %param.8), channel_id=1, replica_groups=mesh['row'=4,'col'=8] {'col'}, dimensions={1}, use_global_device_ids=true | all-gather | bytes 294912 | tf_op jit(solution)/shard_map/all_gather | solution.py:54
  18.7 0.0 copy-done.4
  18.7 0.0 copy-start.2
  18.7 13.7 %all_gather.10 = f32[64,512]{1,0:T(8,128)S(1)} all-gather(f32[64,128]{1,0:T(8,128)S(1)} %copy-done.4), channel_id=1, replica_groups=mesh['row'=4,'col'=8] {'row'}, dimensions={1}, use_global_device_ids=true | all-gather | bytes 163840 | tf_op jit(solution)/shard_map/all_gather | solution.py:59
  33.1 0.0 copy-start.6
  33.1 0.0 copy-done.2
  33.1 0.6 copy-done.6
  33.7 13.2 %all_gather.9 = f32[33,512]{1,0:T(8,128)S(1)} all-gather(f32[33,128]{1,0:T(8,128)S(1)} %pad_maximum_fusion), channel_id=1, replica_groups=mesh['row'=4,'col'=8] {'row'}, dimensions={1}, use_global_device_ids=true | all-gather | bytes 84480 | tf_op jit(solution)/shard_map/all_gather | solution.py:60
  47.1 6.8 %while.13 = (s32[]{:T(128)}, f32[33,1024]{1,0:T(8,128)S(1)}, f32[32,1024]{1,0:T(8,128)S(1)}, f32[4,33,128]{2,1,0:T(8,128)S(1)}, f32[4,64,128]{2,0,1:T(4,128)S(1)...) while((s32[]{:T(128)}, f32[33,1024]{1,0:T(8,128)S(1)}, ...), condition=%wide.region_5.6_spmd.clone, body=%wide.region_3.5_spmd.clone.sunk | while | flops 204228480 | bytes 2569372 | solution.py:41
  47.2 0.7 fusion.20
  47.9 0.5 convolution_add_fusion.4
  48.3 0.5 convolution_add_fusion.5
  48.9 0.7 fusion.20
  49.6 0.5 convolution_add_fusion.4
  50.0 0.5 convolution_add_fusion.5
  50.6 0.7 fusion.20
  51.3 0.5 convolution_add_fusion.4
  51.7 0.5 convolution_add_fusion.5
  52.3 0.7 fusion.20
  53.0 0.5 convolution_add_fusion.4
  53.4 0.5 convolution_add_fusion.5
  53.9 0.0 copy-start.1
  53.9 0.0 copy-start
  53.9 0.6 copy-done.1
  54.6 0.0 reduce-scatter.5.cloned.1.call-update
  54.6 0.0 reduce-scatter.3.cloned.1.call-start
  54.6 0.0 copy-done
  54.6 0.7 reduce-scatter.3.cloned.1.call-update
  56.7 31.4 %reduce-scatter.5.cloned.1.call-done = f32[32,128]{1,0:T(8,128)} async-done(((f32[32,1024]{1,0:T(8,128)}), f32[32,128]{1,0:T(8,128)}) %reduce-scatter.5.cloned.1.call-update) | async-done | bytes 16400 | tf_op jit(solution)/shard_map/reduce_scatter | solution.py:66
  88.1 1.3 broadcast_multiply_fusion.1
  89.4 33.8 %reduce-scatter.3.cloned.1.call-done = f32[33,128]{1,0:T(8,128)} async-done(((f32[33,1024]{1,0:T(8,128)}), f32[33,128]{1,0:T(8,128)}) %reduce-scatter.3.cloned.1.call-update) | async-done | bytes 16912 | tf_op jit(solution)/shard_map/reduce_scatter | solution.py:65
  123.2 0.0 copy-start.3
  123.2 0.9 multiply_reduce_fusion.3
  124.1 39.4 %all-reduce = (f32[33]{0:T(128)S(1)}, f32[33]{0:T(128)S(1)}) all-reduce(f32[33]{0:T(128)S(1)} %get-tuple-element.86, f32[33]{0:T(128)S(1)} %get-tuple-element.85), channel_id=1, replica_groups=mesh['row'=4,'col'=8] {'row','col'}, use_global_device_ids=true, to_apply=%region_1.2 | all-reduce | flops 66 | bytes 528 | tf_op jit(solution)/shard_map/psum | solution.py:72
  163.5 0.0 copy-done.3
  163.5 0.8 multiply_reduce_fusion.2
  164.3 0.0 copy-start.5
  164.3 41.0 %psum.23 = f32[33]{0:T(128)S(1)} all-reduce(f32[33]{0:T(128)S(1)} %get-tuple-element.105), channel_id=1, replica_groups=mesh['row'=4,'col'=8] {'row','col'}, use_global_device_ids=true, to_apply=%region_10.11 | all-reduce | flops 33 | bytes 264 | tf_op jit(solution)/shard_map/psum | solution.py:77
  205.3 0.7 multiply_add_fusion
  206.0 0.0 copy-done.5
  206.0 0.6 slice.12
  (17 shorter events, 0.4 us)
Async XLA Ops:
  7.2 11.6 %copy-start.4 = (f32[64,128]{1,0:T(8,128)S(1)}, f32[64,128]{1,0:T(8,128)}, u32[]{:S(2)}) copy-start(f32[64,128]{1,0:T(8,128)} %param.8) | copy-start | bytes 98308
  7.2 80.9 %reduce-scatter.5.cloned.1.call-start = ((), (), s32[]{:S(2)}) async-start(), calls=%async_computation.3 | async-start | bytes 147456 | tf_op jit(solution)/shard_map/reduce_scatter | solution.py:66
  18.7 14.4 %copy-start.2 = (f32[32,128]{1,0:T(8,128)S(1)}, f32[32,128]{1,0:T(8,128)}, u32[]{:S(2)}) copy-start(f32[32,128]{1,0:T(8,128)} %param.10) | copy-start | bytes 49156
  33.1 0.7 copy-start.6
  53.9 0.6 copy-start.1
  53.9 0.7 copy-start
  54.6 68.6 %reduce-scatter.3.cloned.1.call-start = ((), (), s32[]{:S(2)}) async-start(), calls=%async_computation.2 | async-start | bytes 184320 | tf_op jit(solution)/shard_map/reduce_scatter | solution.py:65
  123.2 40.3 %copy-start.3 = (f32[33,128]{1,0:T(8,128)S(1)}, f32[33,128]{1,0:T(8,128)}, u32[]{:S(2)}) copy-start(f32[33,128]{1,0:T(8,128)} %reduce-scatter.3.cloned.1.call-done) | copy-start | bytes 50692
  164.3 41.7 %copy-start.5 = (f32[33,128]{1,0:T(8,128)}, f32[33,128]{1,0:T(8,128)S(1)}, u32[]{:S(2)}) copy-start(f32[33,128]{1,0:T(8,128)S(1)} %get-tuple-element.106) | copy-start | bytes 50692
Sparse Core Ops, SparseCore 0:
  54.7 33.3 reduce-scatter.4
  91.4 31.7 reduce-scatter.2
where the time goes:
time: 214 us; the launch traced here: 213 us
  blocking collectives  119 us (56%)
  waiting for transfers between devices  65.9 us (31%)
  between operations  16.2 us (8%)
  matrix products  6.39 us (3%)
  other arithmetic  3.86 us (2%)
    psum x1, blocking collectives, shards(): norm_new = lax.psum(jnp.sum(residual * residual, axis=1), ('row', 'col'))  41 us
    psum x1, blocking collectives, shards(): lax.psum((jnp.sum(rhs * rhs, axis=1), jnp.sum(rhs * kb, axis=1)), ('row',...  39.4 us
    reduce_scatter x1, waiting for transfers between devices, shards(): lax.psum_scatter(eb_part, 'col', scatter_dimension=1, tiled=True)  33.8 us
    reduce_scatter x1, waiting for transfers between devices, shards(): lax.psum_scatter(ed_part, 'col', scatter_dimension=1, tiled=True)  31.4 us
    all_gather x1, blocking collectives, shards(): lax.all_gather(points, 'row', axis=1, tiled=True)  13.7 us
    all_gather x1, blocking collectives, shards(): lax.all_gather(rhs, 'row', axis=1, tiled=True)  13.2 us
    all_gather x1, blocking collectives, shards(): row_x = lax.all_gather(points, 'col', axis=1, tiled=True)  11.5 us
  transfers between devices with their start and end apart: 2, of which 2 were waited for; matrix products, arithmetic and copies ran while one was open for 1% of the time, Pallas kernels for 0%

commit v1 on v0

v1 whole, which is shorter than its diff:
```python
import functools

import jax
import jax.numpy as jnp
from jax import lax
from jax.experimental import pallas as pl
from jax.experimental.pallas import tpu as pltpu
from jax.sharding import PartitionSpec as P

MESH = pl.DeviceIdType.MESH
F32 = jnp.float32
BF16 = jnp.bfloat16
NT = (((1,), (1,)), ((), ()))


def up_to(value, multiple):
    return (value + multiple - 1) // multiple * multiple


def split_three(value):
    high = value.astype(BF16)
    rest = value - high.astype(F32)
    middle = rest.astype(BF16)
    low = (rest - middle.astype(F32)).astype(BF16)
    return high, middle, low


def kernel(
    n_row,
    n_quad,
    feats,
    n_probes,
    x_ref,
    t_ref,
    p_ref,
    ls_ref,
    os_ref,
    no_ref,
    sol_ref,
    res_ref,
    dir_ref,
    len_ref,
    scl_ref,
    held,
    mate_block,
    own_split,
    own_sq,
    acc,
    part_out,
    part_in,
    sums,
    recv_sem,
    up_sem,
    down_sem,
    side_sem,
    mate_send,
    mate_recv,
    sum_send,
    sum_recv,
):
    r = lax.axis_index("row")
    col = lax.axis_index("col")
    q = col // 2
    core = col % 2
    n_peers = n_row * n_quad
    me = r * n_quad + q
    width = x_ref.shape[1]
    rhs_rows = up_to(n_probes + 1, 8)
    lhs_rows = up_to(n_probes + 1, 16)
    mate = {"row": r, "col": q * 2 + (1 - core)}

    def device(row, quad):
        return {"row": row, "col": quad * 2 + core}

    barrier = pltpu.get_barrier_semaphore()
    pl.semaphore_signal(barrier, inc=1, device_id=mate, device_id_type=MESH)

    @pl.loop(1, n_peers)
    def _(k):
        peer = (me + k) % n_peers
        pl.semaphore_signal(
            barrier, inc=1, device_id=device(peer // n_quad, peer % n_quad), device_id_type=MESH
        )

    mine = held.at[r, q]
    mine[0:feats, :] = x_ref[...]
    mine[feats : feats + n_probes, :] = p_ref[...]
    mine[feats + n_probes :, :] = jnp.concatenate(
        [t_ref[...], jnp.zeros((rhs_rows - n_probes - 1, width), F32)], 0
    )
    acc[...] = jnp.zeros_like(acc)
    pl.semaphore_wait(barrier, n_peers)

    def copy(src, dst, send, recv, target):
        return pltpu.make_async_remote_copy(
            src_ref=src, dst_ref=dst, send_sem=send, recv_sem=recv, device_id=target, device_id_type=MESH
        )

    def pass_on(row, quad, send, to_row, to_quad):
        slot = held.at[row, quad]
        return copy(slot, slot, send, recv_sem.at[row, quad], device(to_row, to_quad))

    def arrived(row, quad):
        slot = held.at[row, quad]
        copy(slot, slot, mate_send.at[0], recv_sem.at[row, quad], mate).wait_recv()

    paired = jnp.minimum(r, n_row - 1 - r)
    low_side = (2 * r < n_row).astype(jnp.int32)

    def order(t):
        near = r + (t % 2) * (-((t + 1) // 2)) + (1 - t % 2) * (t // 2)
        far = low_side * t + (1 - low_side) * (n_row - 1 - t)
        inside = (t <= 2 * paired).astype(jnp.int32)
        return inside * near + (1 - inside) * far

    def up(row):
        return pass_on(row, q, up_sem.at[row], jnp.minimum(r + 1, n_row - 1), q)

    def down(row):
        return pass_on(row, q, down_sem.at[row], jnp.maximum(r - 1, 0), q)

    def goes_up(row):
        return jnp.logical_and(row <= r, r + 1 < n_row)

    def goes_down(row):
        return jnp.logical_and(row >= r, r >= 1)

    square = n_quad == 4
    near_x = (q // 2) * 2 + (1 - q % 2)
    near_y = (1 - q // 2) * 2 + q % 2
    across = 3 - q

    def side(row, k):
        if square:
            if k == 0:
                return pass_on(row, q, side_sem.at[row, 0], r, near_x)
            if k == 1:
                return pass_on(row, q, side_sem.at[row, 1], r, near_y)
            even = 1 - row % 2
            source = even * near_x + (1 - even) * near_y
            target = even * near_y + (1 - even) * near_x
            return pass_on(row, source, side_sem.at[row, 2], r, target)
        return pass_on(row, q, side_sem.at[row, k], r, (q + k + 1) % n_quad)

    def spread(row):
        @pl.when(goes_up(row))
        def _():
            up(row).start()

        @pl.when(goes_down(row))
        def _():
            down(row).start()

        if square:
            side(row, 0).start()
            side(row, 1).start()
        else:

            @pl.loop(0, n_quad - 1)
            def _(k):
                side(row, k).start()

    to_mate = copy(mine, mate_block, mate_send.at[0], mate_recv.at[0], mate)
    to_mate.start()
    spread(r)

    inv_two = 0.5 / (ls_ref[0] * ls_ref[0])

    def prepare(half, block):
        x = jnp.transpose(block[0:feats, :])
        rows = pl.ds(half * width, width)
        own_sq[rows, :] = jnp.broadcast_to(jnp.sum(x * x, axis=1, keepdims=True), (width, width))
        high, middle, low = split_three(-2.0 * x)
        own_split[rows, :] = jnp.concatenate([high, high, middle, high, low, middle], 1)

    prepare(0, mine)
    to_mate.wait_recv()
    prepare(1, mate_block)

    def absorb(row, quad):
        block = held.at[row, quad]
        x = block[0:feats, :]
        high, middle, low = split_three(x)
        stack = jnp.concatenate([high, middle, high, low, high, middle], 0)
        dots = jnp.dot(own_split[...], stack, preferred_element_type=F32)
        sq = jnp.sum(x * x, axis=0, keepdims=True)
        dist = jnp.maximum((own_sq[...] + sq) + dots, 0.0)
        kern = jnp.exp(dist * (-inv_two))
        both = jnp.concatenate([kern, kern * dist], 0)
        both_high = both.astype(BF16)
        both_middle = (both - both_high.astype(F32)).astype(BF16)
        rhs = jnp.concatenate(
            [block[feats:, :], jnp.zeros((lhs_rows - rhs_rows, width), F32)], 0
        )
        b_high, b_middle, b_low = split_three(rhs)
        first = lax.dot_general(
            jnp.concatenate([b_high, b_middle, b_low], 0), both_high, NT, preferred_element_type=F32
        )
        second = lax.dot_general(
            jnp.concatenate([b_high, b_middle], 0), both_middle, NT, preferred_element_type=F32
        )
        small = (first[2 * lhs_rows :] + second[lhs_rows:]) + (first[lhs_rows : 2 * lhs_rows] + second[:lhs_rows])
        acc[...] += first[:lhs_rows] + small

    def others(row):
        if square:
            arrived(row, near_x)
            arrived(row, near_y)
            side(row, 2).start()
            absorb(row, near_x)
            absorb(row, near_y)
        else:

            @pl.loop(1, n_quad)
            def _(k):
                quad = (q + k) % n_quad
                arrived(row, quad)
                absorb(row, quad)

    def last(row):
        if square:
            arrived(row, across)
            absorb(row, across)

    for t in range(n_row + 2):
        if t < n_row:
            row = order(t)
            if t > 0:
                arrived(row, q)
                spread(row)
            absorb(row, q)
        if 1 <= t <= n_row:
            others(order(t - 1))
        if t >= 2:
            last(order(t - 2))

    part_out[0] = acc[0:rhs_rows, 0:width]
    part_out[1] = acc[0:rhs_rows, width : 2 * width]
    part_out[2] = acc[0:rhs_rows, 3 * width : 4 * width]
    swap = copy(part_out, part_in, mate_send.at[1], mate_recv.at[1], mate)
    swap.start()
    rhs = mine[feats:, :]
    rhs_mate = mate_block[feats:, :]
    scale = os_ref[0]
    noise = no_ref[0]
    norms = rhs * rhs + rhs_mate * rhs_mate
    swap.wait_recv()
    eb = part_out[0] + part_in[1]
    eb_mate = part_out[1] + part_in[0]
    ed = acc[0:rhs_rows, 2 * width : 3 * width] + part_in[2]
    kb = scale * eb + noise * rhs
    kb_mate = scale * eb_mate + noise * rhs_mate
    terms = [norms, rhs * kb + rhs_mate * kb_mate, kb * kb + kb_mate * kb_mate]
    lanes = up_to(3 * rhs_rows, 128)
    if lanes > 3 * rhs_rows:
        terms.append(jnp.zeros((lanes - 3 * rhs_rows, width), F32))
    row_sums = lax.dot_general(
        jnp.ones((8, width), F32),
        jnp.concatenate(terms, 0),
        NT,
        precision=lax.Precision.HIGHEST,
        preferred_element_type=F32,
    )
    sums[me] = row_sums[0:1]

    def share(k):
        peer = (me + k) % n_peers
        return copy(
            sums.at[me], sums.at[me], sum_send.at[peer], sum_recv.at[me],
            device(peer // n_quad, peer % n_quad),
        )

    @pl.loop(1, n_peers)
    def _(k):
        share(k).start()

    scl_ref[...] = eb[0:n_probes]
    len_ref[...] = (scale / (ls_ref[0] * ls_ref[0] * ls_ref[0])) * ed[0:n_probes]

    @pl.loop(1, n_peers)
    def _(k):
        peer = (me + k) % n_peers
        copy(sums.at[peer], sums.at[peer], mate_send.at[0], sum_recv.at[peer], mate).wait_recv()

    total = jnp.sum(sums[...], axis=0)
    lane = lax.broadcasted_iota(jnp.int32, (rhs_rows, lanes), 1)
    sub = lax.broadcasted_iota(jnp.int32, (rhs_rows, lanes), 0)

    def column(index):
        picked = jnp.where(lane == sub + index * rhs_rows, total, 0.0)
        return jnp.sum(picked, axis=1, keepdims=True)

    norm_old, curv, kb_sq = column(0), column(1), column(2)
    alpha = norm_old / curv
    norm_new = jnp.maximum(alpha * (alpha * kb_sq) - norm_old, 0.0)
    beta = norm_new / norm_old
    solved = alpha * rhs
    residual = rhs - alpha * kb
    direction = residual + beta * rhs
    for ref, value in ((sol_ref, solved), (res_ref, residual), (dir_ref, direction)):
        ref[0:1, :] = value[n_probes : n_probes + 1]
        ref[1 : n_probes + 1, :] = value[0:n_probes]

    to_mate.wait_send()
    swap.wait_send()

    @pl.loop(0, n_row)
    def _(row):
        @pl.when(goes_up(row))
        def _():
            up(row).wait_send()

        @pl.when(goes_down(row))
        def _():
            down(row).wait_send()

        if square:
            for k in range(3):
                side(row, k).wait_send()
        else:

            @pl.loop(0, n_quad - 1)
            def _(k):
                side(row, k).wait_send()

    @pl.loop(1, n_peers)
    def _(k):
        share(k).wait_send()


def shards(n_row, n_quad, points, targets, probes, lengthscale, outputscale, noise):
    feats, width = points.shape
    n_probes = probes.shape[0]
    n_peers = n_row * n_quad
    rhs_rows = up_to(n_probes + 1, 8)
    lhs_rows = up_to(n_probes + 1, 16)
    rows = feats + rhs_rows
    vmem = pl.BlockSpec(memory_space=pltpu.VMEM)
    smem = pl.BlockSpec(memory_space=pltpu.SMEM)
    tall = jax.ShapeDtypeStruct((n_probes + 1, width), F32)
    short = jax.ShapeDtypeStruct((n_probes, width), F32)
    return pl.pallas_call(
        functools.partial(kernel, n_row, n_quad, feats, n_probes),
        out_shape=(tall, tall, tall, short, short),
        in_specs=[vmem, vmem, vmem, smem, smem, smem],
        out_specs=(vmem,) * 5,
        scratch_shapes=[
            pltpu.VMEM((n_row, n_quad, rows, width), F32),
            pltpu.VMEM((rows, width), F32),
            pltpu.VMEM((2 * width, 6 * feats), BF16),
            pltpu.VMEM((2 * width, width), F32),
            pltpu.VMEM((lhs_rows, 4 * width), F32),
            pltpu.VMEM((3, rhs_rows, width), F32),
            pltpu.VMEM((3, rhs_rows, width), F32),
            pltpu.VMEM((n_peers, 1, up_to(3 * rhs_rows, 128)), F32),
            pltpu.SemaphoreType.DMA((n_row, n_quad)),
            pltpu.SemaphoreType.DMA((n_row,)),
            pltpu.SemaphoreType.DMA((n_row,)),
            pltpu.SemaphoreType.DMA((n_row, max(n_quad - 1, 3))),
            pltpu.SemaphoreType.DMA((2,)),
            pltpu.SemaphoreType.DMA((2,)),
            pltpu.SemaphoreType.DMA((n_peers,)),
            pltpu.SemaphoreType.DMA((n_peers,)),
        ],
        compiler_params=pltpu.CompilerParams(
            collective_id=0,
            has_side_effects=True,
            vmem_limit_bytes=n_peers * rows * width * 4 + (16 << 20),
        ),
    )(points, targets[None, :], probes, lengthscale, outputscale, noise)


def solution(mesh):
    split = ("row", "col")
    wide = P(None, split)
    return jax.shard_map(
        functools.partial(shards, mesh.shape["row"], mesh.shape["col"] // 2),
        mesh=mesh,
        in_specs=(wide, P(split), wide, P(), P(), P()),
        out_specs=(wide,) * 5,
        check_vma=False,
    )
```

time: 214 us -> 37.1 us (0.17)
  blocking collectives: 119 us -> 0 us
  waiting for transfers between devices: 65.9 us -> 0 us
  Pallas kernels: 0 us -> 29.1 us
  between operations: 16.2 us -> 2.59 us
  matrix products: 6.39 us -> 0 us
  other arithmetic: 3.86 us -> 0 us
  local copies, waits for them, and re-layouts: 2.1 us -> 5.15 us
    psum x2 -> x0, blocking collectives: 80.4 us -> none  [the longest x1 41 us: shards(): norm_new = lax.psum(jnp.sum(residual * residual, axis=1), ('row', 'col'))]
    reduce_scatter x2 -> x0, waiting for transfers between devices: 65.2 us -> none  [the longest x1 33.8 us: shards(): lax.psum_scatter(eb_part, 'col', scatter_dimension=1, tiled=True)]
    all_gather x3 -> x0, blocking collectives: 38.4 us -> none  [the longest x1 13.7 us: shards(): lax.all_gather(points, 'row', axis=1, tiled=True)]
    pallas_call x0 -> x1, Pallas kernels: none -> 29.1 us  [shards(): pl.pallas_call(functools.partial(kernel, n_row, n_quad, feats, n_probes),...]
    dot_general x12 -> x0, matrix products: 6.39 us -> none  [the longest x4 2.67 us: step(): lax.dot_general(x_block, row_x, (((0,), (0,)), ((), ())), precision=lax.P...]
    unnamed x14 -> x11, local copies, waits for them, and re-layouts: 1.29 us -> 5.15 us
  transfers between devices with their start and end apart: 2 -> 0, of which waited for: 2 -> 0; matrix products, arithmetic and copies ran while one was open for 1% -> 0% of each run, Pallas kernels for 0% -> 0%
where the time goes in v1:
time: 37.1 us; the launch traced here: 36.8 us
  Pallas kernels  29.1 us (78%)
  local copies, waits for them, and re-layouts  5.15 us (14%)
  between operations  2.59 us (7%)
    pallas_call x1, Pallas kernels, shards(): pl.pallas_call(functools.partial(kernel, n_row, n_quad, feats, n_probes),...  29.1 us
    unnamed x11, local copies, waits for them, and re-layouts  5.15 us

profile of v1, /device:TPU:0, one launch (start us, length us, event | category | flops | bytes accessed | tf_op | source)
XLA Modules:
  0.0 36.8 jit_solution(18184889431218266766)
XLA Ops:
  2.6 0.0 copy-start.2
  2.6 0.6 %copy-done.2 = f32[128]{0:T(128)S(1)} copy-done((f32[128]{0:T(128)S(1)}, f32[128]{0:T(128)}, u32[]{:S(2)}) %copy-start.2) | copy-done | bytes 536
  3.2 0.0 copy-start
  3.2 0.8 %copy-done = f32[64,128]{1,0:T(8,128)S(1)} copy-done((f32[64,128]{1,0:T(8,128)S(1)}, f32[64,128]{1,0:T(8,128)}, u32[]{:S(2)}) %copy-start) | copy-done | bytes 32792
  4.0 0.0 copy-start.1
  4.0 0.7 %copy-done.1 = f32[32,128]{1,0:T(8,128)S(1)} copy-done((f32[32,128]{1,0:T(8,128)S(1)}, f32[32,128]{1,0:T(8,128)}, u32[]{:S(2)}) %copy-start.1) | copy-done | bytes 16408
  4.7 29.1 %shard_map.101 = (f32[33,128]{1,0:T(8,128)S(1)}, f32[33,128]{1,0:T(8,128)S(1)}, f32[33,128]{1,0:T(8,128)S(1)}, f32[32,128]{1,0:T(8,128)S(1)}, f32[32,128]{1,0:T(8,128)S(1)}) custom-call(f32[64,128]{1,0:T(8,128)S(1)} %copy-done, f32[1,128]{1,0:T(1,128)S(1)} %bitcast.1, f32[32,128]{1,0:T(8,128)S(1)} %copy-done.1, f32[1]{0:T(128)S(6)} %copy.16.ls_ref, ...), custom_call_target="tpu_custom_call" | custom-call | tf_op jit(solution)/shard_map/pallas_call | solution.py:342
  33.8 0.6 %copy.19 = f32[33,128]{1,0:T(8,128)} copy(f32[33,128]{1,0:T(8,128)S(1)} %get-tuple-element.10) | data formatting | bytes 33792
  34.4 0.6 %copy.20 = f32[33,128]{1,0:T(8,128)} copy(f32[33,128]{1,0:T(8,128)S(1)} %get-tuple-element.11) | data formatting | bytes 33792
  35.0 0.6 %copy.21 = f32[33,128]{1,0:T(8,128)} copy(f32[33,128]{1,0:T(8,128)S(1)} %get-tuple-element.12) | data formatting | bytes 33792
  35.6 0.6 %copy.22 = f32[32,128]{1,0:T(8,128)} copy(f32[32,128]{1,0:T(8,128)S(1)} %get-tuple-element.13) | data formatting | bytes 32768
  36.2 0.6 %copy.23 = f32[32,128]{1,0:T(8,128)} copy(f32[32,128]{1,0:T(8,128)S(1)} %get-tuple-element.14) | data formatting | bytes 32768
Async XLA Ops:
  2.6 0.7 %copy-start.2 = (f32[128]{0:T(128)S(1)}, f32[128]{0:T(128)}, u32[]{:S(2)}) copy-start(f32[128]{0:T(128)} %param.7) | copy-start | bytes 1540
  3.2 0.8 %copy-start = (f32[64,128]{1,0:T(8,128)S(1)}, f32[64,128]{1,0:T(8,128)}, u32[]{:S(2)}) copy-start(f32[64,128]{1,0:T(8,128)} %x_ref.1) | copy-start | bytes 98308
  4.0 0.7 %copy-start.1 = (f32[32,128]{1,0:T(8,128)S(1)}, f32[32,128]{1,0:T(8,128)}, u32[]{:S(2)}) copy-start(f32[32,128]{1,0:T(8,128)} %p_ref.1) | copy-start | bytes 49156

commit v2 on v0

v2 whole, which is shorter than its diff:
```python
import functools

import jax
import jax.numpy as jnp
from jax import lax
from jax.experimental import pallas as pl
from jax.experimental.pallas import tpu as pltpu
from jax.sharding import PartitionSpec as P

MESH = pl.DeviceIdType.MESH
F32 = jnp.float32
BF16 = jnp.bfloat16
NT = (((1,), (1,)), ((), ()))


def up_to(value, multiple):
    return (value + multiple - 1) // multiple * multiple


def split_three(value):
    high = value.astype(BF16)
    rest = value - high.astype(F32)
    middle = rest.astype(BF16)
    low = (rest - middle.astype(F32)).astype(BF16)
    return high, middle, low


def kernel(
    n_row,
    n_col,
    feats,
    n_probes,
    x_hbm,
    t_hbm,
    p_hbm,
    ls_ref,
    os_ref,
    no_ref,
    sol_hbm,
    res_hbm,
    dir_hbm,
    len_hbm,
    scl_hbm,
    held,
    plane,
    targets,
    own_split,
    own_sq,
    acc,
    part_out,
    part_in,
    line_sums,
    plane_sums,
    load_sem,
    line_send,
    line_recv,
    plane_send,
    plane_recv,
    part_send,
    part_recv,
    ls_send,
    ls_recv,
    ps_send,
    ps_recv,
    tall_out,
    short_out,
    store_sem,
):
    r = lax.axis_index("row")
    col = lax.axis_index("col")
    n_quad = n_col // 2
    q = col // 2
    width = x_hbm.shape[1]
    rhs_rows = up_to(n_probes + 1, 8)
    lhs_rows = up_to(n_probes + 1, 16)

    mine = held.at[r]
    loads = [
        pltpu.make_async_copy(x_hbm, mine.at[0:feats], load_sem.at[0]),
        pltpu.make_async_copy(p_hbm, mine.at[feats : feats + n_probes], load_sem.at[1]),
        pltpu.make_async_copy(t_hbm, targets, load_sem.at[2]),
    ]
    for load in loads:
        load.start()

    barrier = pltpu.get_barrier_semaphore()

    def on_line(k):
        return (r + k) % n_row

    def on_plane(k):
        return (col + k) % n_col

    @pl.loop(1, n_row)
    def _(k):
        pl.semaphore_signal(
            barrier, inc=1, device_id={"row": on_line(k), "col": col}, device_id_type=MESH
        )

    @pl.loop(1, n_col)
    def _(k):
        pl.semaphore_signal(
            barrier, inc=1, device_id={"row": r, "col": on_plane(k)}, device_id_type=MESH
        )

    acc[...] = jnp.zeros_like(acc)
    for load in loads:
        load.wait()
    mine[feats + n_probes :, :] = jnp.concatenate(
        [targets[...], jnp.zeros((rhs_rows - n_probes - 1, width), F32)], 0
    )
    pl.semaphore_wait(barrier, n_row + n_col - 2)

    def copy(src, dst, send, recv, row, column):
        return pltpu.make_async_remote_copy(
            src_ref=src, dst_ref=dst, send_sem=send, recv_sem=recv,
            device_id={"row": row, "col": column}, device_id_type=MESH,
        )

    paired = jnp.minimum(r, n_row - 1 - r)
    low_side = (2 * r < n_row).astype(jnp.int32)

    def order(t):
        near = r + (t % 2) * (-((t + 1) // 2)) + (1 - t % 2) * (t // 2)
        far = low_side * t + (1 - low_side) * (n_row - 1 - t)
        inside = (t <= 2 * paired).astype(jnp.int32)
        return inside * near + (1 - inside) * far

    def block_to(row):
        return copy(mine, held.at[r], line_send.at[row], line_recv.at[r], row, col)

    def feats_to(column):
        return copy(
            mine.at[0:feats], plane.at[col], plane_send.at[column], plane_recv.at[col], r, column
        )

    def block_from(row):
        slot = held.at[row]
        return copy(slot, slot, line_send.at[row], line_recv.at[row], row, col)

    def feats_from(column):
        slot = plane.at[column]
        return copy(slot, slot, plane_send.at[column], plane_recv.at[column], r, column)

    def part_to(column):
        return copy(
            part_out.at[column], part_in.at[col], part_send.at[column], part_recv.at[col], r, column
        )

    def part_from(column):
        slot = part_in.at[column]
        return copy(slot, slot, part_send.at[column], part_recv.at[column], r, column)

    mate = q * 2 + (1 - col % 2)
    block_to(order(1)).start()
    feats_to(mate).start()

    @pl.loop(2, n_row)
    def _(t):
        block_to(order(t)).start()

    @pl.loop(1, n_col)
    def _(k):
        @pl.when(on_plane(k) != mate)
        def _():
            feats_to(on_plane(k)).start()

    plane[col] = mine[0:feats, :]
    inv_two = 0.5 / (ls_ref[0] * ls_ref[0])

    def chunk(k):
        if n_quad != 4:
            return (q + k) % n_quad
        x, y = q % 2, q // 2
        return (q, y * 2 + 1 - x, (1 - y) * 2 + x, 3 - q)[k]

    def each_chunk(use, backwards=False):
        if n_quad == 4:
            for k in (3, 2, 1, 0) if backwards else range(4):
                use(chunk(k), k == 0)
        else:
            use(q, True)

            @pl.loop(1, n_quad)
            def _(k):
                use(chunk(k), False)

    def prepare(quad):
        for half in range(2):
            x = jnp.transpose(plane[2 * quad + half])
            rows = slice(half * width, (half + 1) * width)
            own_sq[quad, rows, :] = jnp.broadcast_to(
                jnp.sum(x * x, axis=1, keepdims=True), (width, width)
            )
            high, middle, low = split_three(-2.0 * x)
            own_split[quad, rows, :] = jnp.concatenate([high, high, middle, high, low, middle], 1)

    def open_block(row):
        block = held.at[row]
        x = block[0:feats, :]
        high, middle, low = split_three(x)
        stack = jnp.concatenate([high, middle, high, low, high, middle], 0)
        sq = jnp.sum(x * x, axis=0, keepdims=True)
        rhs = jnp.concatenate(
            [block[feats:, :], jnp.zeros((lhs_rows - rhs_rows, width), F32)], 0
        )
        b_high, b_middle, b_low = split_three(rhs)
        return (
            stack,
            sq,
            jnp.concatenate([b_high, b_middle, b_low], 0),
            jnp.concatenate([b_high, b_middle], 0),
        )

    def absorb(opened, quad):
        stack, sq, lhs_three, lhs_two = opened
        dots = jnp.dot(own_split[quad], stack, preferred_element_type=F32)
        dist = jnp.maximum((own_sq[quad] + sq) + dots, 0.0)
        kern = jnp.exp(dist * (-inv_two))
        both = jnp.concatenate([kern, kern * dist], 0)
        both_high = both.astype(BF16)
        both_middle = (both - both_high.astype(F32)).astype(BF16)
        first = lax.dot_general(lhs_three, both_high, NT, preferred_element_type=F32)
        second = lax.dot_general(lhs_two, both_middle, NT, preferred_element_type=F32)
        small = (first[2 * lhs_rows :] + second[lhs_rows:]) + (
            first[lhs_rows : 2 * lhs_rows] + second[:lhs_rows]
        )
        acc[quad] += first[:lhs_rows] + small

    def send_parts(quad, is_own):
        for half in range(2):
            column = 2 * quad + half
            part_out[column, 0:rhs_rows, :] = acc[quad, 0:rhs_rows, half * width : (half + 1) * width]
            part_out[column, rhs_rows:, :] = acc[
                quad, 0:n_probes, (2 + half) * width : (3 + half) * width
            ]
        if is_own:
            part_to(mate).start()
        else:
            part_to(2 * quad).start()
            part_to(2 * quad + 1).start()

    opened = open_block(r)

    def first_use(quad, is_own):
        if is_own:
            feats_from(mate).wait_recv()
        else:
            feats_from(2 * quad).wait_recv()
            feats_from(2 * quad + 1).wait_recv()
        prepare(quad)
        absorb(opened, quad)
        if n_row == 1:
            send_parts(quad, is_own)

    each_chunk(first_use)
    for t in range(1, n_row):
        row = order(t)
        block_from(row).wait_recv()
        opened = open_block(row)

        def use(quad, is_own, opened=opened, last=t == n_row - 1):
            absorb(opened, quad)
            if last:
                send_parts(quad, is_own)

        each_chunk(use, backwards=True)

    part_in[col] = part_out[col]
    rhs = mine[feats:, :]
    scale = os_ref[0]
    noise = no_ref[0]

    @pl.loop(1, n_col)
    def _(k):
        part_from(on_plane(k)).wait_recv()

    whole = jnp.sum(part_in[...], axis=0)
    eb = whole[0:rhs_rows]
    ed = whole[rhs_rows:]
    kb = scale * eb + noise * rhs
    terms = [rhs * rhs, rhs * kb, kb * kb]
    lanes = up_to(3 * rhs_rows, 128)
    if lanes > 3 * rhs_rows:
        terms.append(jnp.zeros((lanes - 3 * rhs_rows, width), F32))
    row_sums = lax.dot_general(
        jnp.ones((8, width), F32),
        jnp.concatenate(terms, 0),
        NT,
        precision=lax.Precision.HIGHEST,
        preferred_element_type=F32,
    )
    line_sums[r] = row_sums[0:1]

    def line_share(k):
        row = on_line(k)
        return copy(line_sums.at[r], line_sums.at[r], ls_send.at[row], ls_recv.at[r], row, col)

    def plane_share(k):
        column = on_plane(k)
        return copy(
            plane_sums.at[col], plane_sums.at[col], ps_send.at[column], ps_recv.at[col], r, column
        )

    for k in range(1, n_row):
        line_share(k).start()

    tall = n_probes + 1
    short_out[0] = (scale / (ls_ref[0] * ls_ref[0] * ls_ref[0])) * ed
    short_out[1] = eb[0:n_probes]
    stores = [
        pltpu.make_async_copy(tall_out.at[0], sol_hbm, store_sem.at[0]),
        pltpu.make_async_copy(tall_out.at[1], res_hbm, store_sem.at[1]),
        pltpu.make_async_copy(tall_out.at[2], dir_hbm, store_sem.at[2]),
        pltpu.make_async_copy(short_out.at[0], len_hbm, store_sem.at[3]),
        pltpu.make_async_copy(short_out.at[1], scl_hbm, store_sem.at[4]),
    ]
    stores[3].start()
    stores[4].start()

    @pl.loop(1, n_row)
    def _(k):
        row = on_line(k)
        slot = line_sums.at[row]
        copy(slot, slot, ls_send.at[row], ls_recv.at[row], row, col).wait_recv()

    plane_sums[col] = jnp.sum(line_sums[...], axis=0)

    @pl.loop(1, n_col)
    def _(k):
        plane_share(k).start()

    @pl.loop(1, n_col)
    def _(k):
        column = on_plane(k)
        slot = plane_sums.at[column]
        copy(slot, slot, ps_send.at[column], ps_recv.at[column], r, column).wait_recv()

    total = jnp.sum(plane_sums[...], axis=0)
    lane = lax.broadcasted_iota(jnp.int32, (rhs_rows, lanes), 1)
    sub = lax.broadcasted_iota(jnp.int32, (rhs_rows, lanes), 0)

    def column_of(index):
        picked = jnp.where(lane == sub + index * rhs_rows, total, 0.0)
        return jnp.sum(picked, axis=1, keepdims=True)

    norm_old, curv, kb_sq = column_of(0), column_of(1), column_of(2)
    alpha = norm_old / curv
    norm_new = jnp.maximum(alpha * (alpha * kb_sq) - norm_old, 0.0)
    beta = norm_new / norm_old
    residual = rhs - alpha * kb
    for index, value in enumerate((alpha * rhs, residual, residual + beta * rhs)):
        tall_out[index, 0:1, :] = value[n_probes:tall]
        tall_out[index, 1:tall, :] = value[0:n_probes]
        stores[index].start()

    @pl.loop(1, n_row)
    def _(k):
        block_to(on_line(k)).wait_send()
        line_share(k).wait_send()

    @pl.loop(1, n_col)
    def _(k):
        feats_to(on_plane(k)).wait_send()
        part_to(on_plane(k)).wait_send()
        plane_share(k).wait_send()

    for store in stores:
        store.wait()


def hand_over(n_arrays, *refs):
    moves = [
        pltpu.make_async_copy(refs[i], refs[n_arrays + i], refs[2 * n_arrays].at[i])
        for i in range(n_arrays)
    ]
    for move in moves:
        move.start()
    for move in moves:
        move.wait()


def shards(n_row, n_col, points, targets, probes, lengthscale, outputscale, noise):
    feats, width = points.shape
    n_probes = probes.shape[0]
    n_quad = n_col // 2
    rhs_rows = up_to(n_probes + 1, 8)
    lhs_rows = up_to(n_probes + 1, 16)
    rows = feats + rhs_rows
    lanes = up_to(3 * rhs_rows, 128)
    smem = pl.BlockSpec(memory_space=pltpu.SMEM)
    hbm = pl.BlockSpec(memory_space=pltpu.HBM)
    dma = pltpu.SemaphoreType.DMA
    tall = jax.ShapeDtypeStruct((n_probes + 1, width), F32)
    short = jax.ShapeDtypeStruct((n_probes, width), F32)
    outs = (tall, tall, tall, short, short)
    results = pl.pallas_call(
        functools.partial(kernel, n_row, n_col, feats, n_probes),
        out_shape=outs,
        in_specs=[hbm, hbm, hbm, smem, smem, smem],
        out_specs=(hbm,) * len(outs),
        scratch_shapes=[
            pltpu.VMEM((n_row, rows, width), F32),
            pltpu.VMEM((n_col, feats, width), F32),
            pltpu.VMEM((1, width), F32),
            pltpu.VMEM((n_quad, 2 * width, 6 * feats), BF16),
            pltpu.VMEM((n_quad, 2 * width, width), F32),
            pltpu.VMEM((n_quad, lhs_rows, 4 * width), F32),
            pltpu.VMEM((n_col, rhs_rows + n_probes, width), F32),
            pltpu.VMEM((n_col, rhs_rows + n_probes, width), F32),
            pltpu.VMEM((n_row, 1, lanes), F32),
            pltpu.VMEM((n_col, 1, lanes), F32),
            dma((3,)),
            dma((n_row,)),
            dma((n_row,)),
            dma((n_col,)),
            dma((n_col,)),
            dma((n_col,)),
            dma((n_col,)),
            dma((n_row,)),
            dma((n_row,)),
            dma((n_col,)),
            dma((n_col,)),
            pltpu.VMEM((3, n_probes + 1, width), F32),
            pltpu.VMEM((2, n_probes, width), F32),
            dma((len(outs),)),
        ],
        compiler_params=pltpu.CompilerParams(
            collective_id=0, has_side_effects=True, vmem_limit_bytes=60 << 20
        ),
    )(points, targets[None, :], probes, lengthscale, outputscale, noise)
    return pl.pallas_call(
        functools.partial(hand_over, len(outs)),
        out_shape=outs,
        in_specs=[hbm] * len(outs),
        out_specs=(hbm,) * len(outs),
        scratch_shapes=[dma((len(outs),))],
        compiler_params=pltpu.CompilerParams(vmem_limit_bytes=60 << 20),
    )(*results)


def solution(mesh):
    split = ("row", "col")
    wide = P(None, split)
    return jax.shard_map(
        functools.partial(shards, mesh.shape["row"], mesh.shape["col"]),
        mesh=mesh,
        in_specs=(wide, P(split), wide, P(), P(), P()),
        out_specs=(wide,) * 5,
        check_vma=False,
    )
```

time: 214 us -> 33.5 us (0.16)
  blocking collectives: 119 us -> 0 us
  waiting for transfers between devices: 65.9 us -> 0 us
  Pallas kernels: 0 us -> 30.7 us
  between operations: 16.2 us -> 2.58 us
  matrix products: 6.39 us -> 0 us
  other arithmetic: 3.86 us -> 0 us
    psum x2 -> x0, blocking collectives: 80.4 us -> none  [the longest x1 41 us: shards(): norm_new = lax.psum(jnp.sum(residual * residual, axis=1), ('row', 'col'))]
    reduce_scatter x2 -> x0, waiting for transfers between devices: 65.2 us -> none  [the longest x1 33.8 us: shards(): lax.psum_scatter(eb_part, 'col', scatter_dimension=1, tiled=True)]
    all_gather x3 -> x0, blocking collectives: 38.4 us -> none  [the longest x1 13.7 us: shards(): lax.all_gather(points, 'row', axis=1, tiled=True)]
    pallas_call x0 -> x2, Pallas kernels: none -> 30.7 us  [the longest x1 27.1 us: shards(): pl.pallas_call(functools.partial(kernel, n_row, n_col, feats, n_probes),...]
    dot_general x12 -> x0, matrix products: 6.39 us -> none  [the longest x4 2.67 us: step(): lax.dot_general(x_block, row_x, (((0,), (0,)), ((), ())), precision=lax.P...]
  transfers between devices with their start and end apart: 2 -> 0, of which waited for: 2 -> 0; matrix products, arithmetic and copies ran while one was open for 1% -> 0% of each run, Pallas kernels for 0% -> 0%
where the time goes in v2:
time: 33.5 us; the launch traced here: 33.3 us
  Pallas kernels  30.7 us (92%)
  between operations  2.58 us (8%)
    pallas_call x1, Pallas kernels, shards(): pl.pallas_call(functools.partial(kernel, n_row, n_col, feats, n_probes),...  27.1 us
    pallas_call x1, Pallas kernels, shards(): pl.pallas_call(functools.partial(hand_over, len(outs)), out_shape=outs, i...  3.68 us

profile of v2, /device:TPU:0, one launch (start us, length us, event | category | flops | bytes accessed | tf_op | source)
XLA Modules:
  0.0 33.3 jit_solution(5069376123716891058)
XLA Ops:
  2.6 27.1 %shard_map.101 = (f32[33,128]{1,0:T(8,128)}, f32[33,128]{1,0:T(8,128)}, f32[33,128]{1,0:T(8,128)}, f32[32,128]{1,0:T(8,128)}, f32[32,128]{1,0:T(8,128)}) custom-call(f32[64,128]{1,0:T(8,128)} %x_hbm.1, f32[1,128]{1,0:T(1,128)} %bitcast.1, f32[32,128]{1,0:T(8,128)} %p_hbm.1, f32[1]{0:T(128)S(6)} %copy.11.ls_ref, f32[1]{0:T(128)S(6)} %copy.12.os_ref, ...), custom_call_target="tpu_custom_call" | custom-call | tf_op jit(solution)/shard_map/pallas_call | solution.py:397
  29.6 3.7 %shard_map.102 = (f32[33,128]{1,0:T(8,128)}, f32[33,128]{1,0:T(8,128)}, f32[33,128]{1,0:T(8,128)}, f32[32,128]{1,0:T(8,128)}, f32[32,128]{1,0:T(8,128)}) custom-call(f32[33,128]{1,0:T(8,128)} %get-tuple-element.10.refs_0_, f32[33,128]{1,0:T(8,128)} %get-tuple-element.11.refs_1_, f32[33,128]{1,0:T(8,128)} %get-tuple-element.12.refs_2_, ...), custom_call_target="tpu_custom_call" | custom-call | tf_op jit(solution)/shard_map/pallas_call | solution.py:432

commit v3 on v2

v3 whole, which is shorter than its diff:
```python
import functools

import jax
import jax.numpy as jnp
from jax import lax
from jax.experimental import pallas as pl
from jax.experimental.pallas import tpu as pltpu
from jax.sharding import PartitionSpec as P

MESH = pl.DeviceIdType.MESH
F32 = jnp.float32
BF16 = jnp.bfloat16
NT = (((1,), (1,)), ((), ()))


def up_to(value, multiple):
    return (value + multiple - 1) // multiple * multiple


def split_three(value):
    high = value.astype(BF16)
    rest = value - high.astype(F32)
    middle = rest.astype(BF16)
    low = (rest - middle.astype(F32)).astype(BF16)
    return high, middle, low


def each(first, last, use):
    if last - first <= 7:
        for k in range(first, last):
            use(k)
    else:
        pl.loop(first, last)(use)


def kernel(
    n_row,
    n_col,
    feats,
    n_probes,
    x_hbm,
    t_hbm,
    p_hbm,
    ls_ref,
    os_ref,
    no_ref,
    out_ref,
    held,
    other,
    plane,
    targets,
    own_split,
    own_sq,
    acc,
    part_out,
    part_in,
    line_sums,
    plane_sums,
    load_sem,
    line_send,
    line_recv,
    mate_send,
    mate_recv,
    plane_send,
    plane_recv,
    part_send,
    part_recv,
    ls_send,
    ls_recv,
    ps_send,
    ps_recv,
):
    r = lax.axis_index("row")
    col = lax.axis_index("col")
    n_quad = n_col // 2
    q = col // 2
    width = x_hbm.shape[1]
    rhs_rows = up_to(n_probes + 1, 8)
    lhs_rows = up_to(n_probes + 1, 16)

    mine = held.at[r]
    loads = [
        pltpu.make_async_copy(x_hbm, mine.at[0:feats], load_sem.at[0]),
        pltpu.make_async_copy(p_hbm, mine.at[feats : feats + n_probes], load_sem.at[1]),
        pltpu.make_async_copy(t_hbm, targets, load_sem.at[2]),
    ]
    for load in loads:
        load.start()

    barrier = pltpu.get_barrier_semaphore()

    def on_line(k):
        return (r + k) % n_row

    def on_plane(k):
        return (col + k) % n_col

    def greet(row, column):
        pl.semaphore_signal(
            barrier, inc=1, device_id={"row": row, "col": column}, device_id_type=MESH
        )

    each(1, n_row, lambda k: greet(on_line(k), col))
    each(1, n_col, lambda k: greet(r, on_plane(k)))

    acc[...] = jnp.zeros_like(acc)
    for load in loads:
        load.wait()
    mine[feats + n_probes :, :] = jnp.concatenate(
        [targets[...], jnp.zeros((rhs_rows - n_probes - 1, width), F32)], 0
    )
    pl.semaphore_wait(barrier, n_row + n_col - 2)

    def copy(src, dst, send, recv, row, column):
        return pltpu.make_async_remote_copy(
            src_ref=src, dst_ref=dst, send_sem=send, recv_sem=recv,
            device_id={"row": row, "col": column}, device_id_type=MESH,
        )

    paired = jnp.minimum(r, n_row - 1 - r)
    low_side = (2 * r < n_row).astype(jnp.int32)

    def order(t):
        near = r + (t % 2) * (-((t + 1) // 2)) + (1 - t % 2) * (t // 2)
        far = low_side * t + (1 - low_side) * (n_row - 1 - t)
        inside = (t <= 2 * paired).astype(jnp.int32)
        return inside * near + (1 - inside) * far

    def block_to(row):
        return copy(mine, held.at[r], line_send.at[row], line_recv.at[r], row, col)

    def block_from(row):
        slot = held.at[row]
        return copy(slot, slot, line_send.at[row], line_recv.at[row], row, col)

    mate = q * 2 + (1 - col % 2)

    def to_mate(row):
        return copy(held.at[row], other.at[row], mate_send.at[row], mate_recv.at[row], r, mate)

    def feats_to(quad):
        return copy(
            mine.at[0:feats], plane.at[q], plane_send.at[quad], plane_recv.at[q],
            r, quad * 2 + col % 2,
        )

    def feats_from(quad):
        slot = plane.at[quad]
        return copy(slot, slot, plane_send.at[quad], plane_recv.at[quad], r, quad * 2 + col % 2)

    def part_to(quad):
        return copy(
            part_out.at[quad], part_in.at[q], part_send.at[quad], part_recv.at[q],
            r, quad * 2 + col % 2,
        )

    def part_from(quad):
        slot = part_in.at[quad]
        return copy(slot, slot, part_send.at[quad], part_recv.at[quad], r, quad * 2 + col % 2)

    def chunk(k):
        if n_quad != 4:
            return (q + k) % n_quad
        x, y = q % 2, q // 2
        return (q, y * 2 + 1 - x, (1 - y) * 2 + x, 3 - q)[k]

    to_mate(r).start()
    block_to(order(1)).start()
    each(1, n_quad, lambda k: feats_to(chunk(k)).start())
    each(2, n_row, lambda t: block_to(order(t)).start())
    plane[q] = mine[0:feats, :]
    inv_two = 0.5 / (ls_ref[0] * ls_ref[0])

    def prepare(k):
        x = jnp.transpose(plane[chunk(k)])
        rows = pl.ds(pl.multiple_of(k * width, width), width)
        own_sq[rows, :] = jnp.broadcast_to(
            jnp.sum(x * x, axis=1, keepdims=True), (width, 2 * width)
        )
        high, middle, low = split_three(-2.0 * x)
        own_split[rows, :] = jnp.concatenate([high, high, middle, high, low, middle], 1)

    def open_pair(row):
        x = jnp.concatenate([held[row, 0:feats, :], other[row, 0:feats, :]], 1)
        high, middle, low = split_three(x)
        stack = jnp.concatenate([high, middle, high, low, high, middle], 0)
        sq = jnp.sum(x * x, axis=0, keepdims=True)
        rhs = jnp.concatenate([held[row, feats:, :], other[row, feats:, :]], 1)
        rhs = jnp.concatenate([rhs, jnp.zeros((lhs_rows - rhs_rows, 2 * width), F32)], 0)
        b_high, b_middle, b_low = split_three(rhs)
        return (
            stack,
            sq,
            jnp.concatenate([b_high, b_middle, b_low], 0),
            jnp.concatenate([b_high, b_middle], 0),
        )

    group = 2 if n_quad % 2 == 0 else 1
    span = group * width

    def absorb(opened, index):
        stack, sq, lhs_three, lhs_two = opened
        rows = pl.ds(pl.multiple_of(index * span, span), span)
        dots = jnp.dot(own_split[rows, :], stack, preferred_element_type=F32)
        dist = jnp.maximum((own_sq[rows, :] + sq) + dots, 0.0)
        kern = jnp.exp(dist * (-inv_two))
        both = jnp.concatenate([kern, kern * dist], 0)
        both_high = both.astype(BF16)
        both_middle = (both - both_high.astype(F32)).astype(BF16)
        first = lax.dot_general(lhs_three, both_high, NT, preferred_element_type=F32)
        second = lax.dot_general(lhs_two, both_middle, NT, preferred_element_type=F32)
        small = (first[2 * lhs_rows :] + second[lhs_rows:]) + (
            first[lhs_rows : 2 * lhs_rows] + second[:lhs_rows]
        )
        acc[index] += first[:lhs_rows] + small

    def send_parts(index, own_too):
        for j in range(group):
            quad = chunk(index * group + j)
            part_out[quad, 0:rhs_rows, :] = acc[index, 0:rhs_rows, j * width : (j + 1) * width]
            part_out[quad, rhs_rows:, :] = acc[
                index, 0:n_probes, span + j * width : span + (j + 1) * width
            ]
            if not (own_too and j == 0):
                part_to(quad).start()

    prepare(0)

    def prepare_other(k):
        feats_from(chunk(k)).wait_recv()
        prepare(k)

    each(1, n_quad, prepare_other)
    n_groups = n_quad // group
    for t in range(n_row):
        if t + 1 < n_row:
            block_from(order(t + 1)).wait_recv()
            to_mate(order(t + 1)).start()
        row = order(t)
        arrival = other.at[row]
        copy(arrival, arrival, mate_send.at[row], mate_recv.at[row], r, mate).wait_recv()
        opened = open_pair(row)
        if t < n_row - 1:
            each(0, n_groups, lambda index: absorb(opened, index))
        else:

            def finish(index, own_too=False):
                absorb(opened, index)
                send_parts(index, own_too)

            each(1, n_groups, finish)
            finish(0, True)

    part_in[q] = part_out[q]
    rhs = mine[feats:, :]
    scale = os_ref[0]
    noise = no_ref[0]

    each(1, n_quad, lambda k: part_from(chunk(k)).wait_recv())

    whole = jnp.sum(part_in[...], axis=0)
    eb = whole[0:rhs_rows]
    ed = whole[rhs_rows:]
    kb = scale * eb + noise * rhs
    terms = [rhs * rhs, rhs * kb, kb * kb]
    lanes = up_to(3 * rhs_rows, 128)
    if lanes > 3 * rhs_rows:
        terms.append(jnp.zeros((lanes - 3 * rhs_rows, width), F32))
    row_sums = lax.dot_general(
        jnp.ones((8, width), F32),
        jnp.concatenate(terms, 0),
        NT,
        precision=lax.Precision.HIGHEST,
        preferred_element_type=F32,
    )
    line_sums[r] = row_sums[0:1]

    def line_share(k):
        row = on_line(k)
        return copy(line_sums.at[r], line_sums.at[r], ls_send.at[row], ls_recv.at[r], row, col)

    def plane_share(k):
        column = on_plane(k)
        return copy(
            plane_sums.at[col], plane_sums.at[col], ps_send.at[column], ps_recv.at[col], r, column
        )

    each(1, n_row, lambda k: line_share(k).start())

    tall = n_probes + 1
    out_ref[3, 0:n_probes, :] = (scale / (ls_ref[0] * ls_ref[0] * ls_ref[0])) * ed
    out_ref[4, 0:n_probes, :] = eb[0:n_probes]

    def line_arrived(k):
        row = on_line(k)
        slot = line_sums.at[row]
        copy(slot, slot, ls_send.at[row], ls_recv.at[row], row, col).wait_recv()

    each(1, n_row, line_arrived)

    plane_sums[col] = jnp.sum(line_sums[...], axis=0)

    each(1, n_col, lambda k: plane_share(k).start())

    def plane_arrived(k):
        column = on_plane(k)
        slot = plane_sums.at[column]
        copy(slot, slot, ps_send.at[column], ps_recv.at[column], r, column).wait_recv()

    each(1, n_col, plane_arrived)

    total = jnp.sum(plane_sums[...], axis=0)
    lane = lax.broadcasted_iota(jnp.int32, (rhs_rows, lanes), 1)
    sub = lax.broadcasted_iota(jnp.int32, (rhs_rows, lanes), 0)

    def column_of(index):
        picked = jnp.where(lane == sub + index * rhs_rows, total, 0.0)
        return jnp.sum(picked, axis=1, keepdims=True)

    norm_old, curv, kb_sq = column_of(0), column_of(1), column_of(2)
    alpha = norm_old / curv
    norm_new = jnp.maximum(alpha * (alpha * kb_sq) - norm_old, 0.0)
    beta = norm_new / norm_old
    residual = rhs - alpha * kb
    for index, value in enumerate((alpha * rhs, residual, residual + beta * rhs)):
        out_ref[index, 0:1, :] = value[n_probes:tall]
        out_ref[index, 1:tall, :] = value[0:n_probes]

    def line_left(k):
        block_to(on_line(k)).wait_send()
        line_share(k).wait_send()

    def quad_left(k):
        feats_to(chunk(k)).wait_send()
        part_to(chunk(k)).wait_send()

    each(1, n_row, line_left)
    each(0, n_row, lambda row: to_mate(row).wait_send())
    each(1, n_quad, quad_left)
    each(1, n_col, lambda k: plane_share(k).wait_send())


def unpack(packed, sol_ref, res_ref, dir_ref, len_ref, scl_ref):
    for index, ref in enumerate((sol_ref, res_ref, dir_ref, len_ref, scl_ref)):
        ref[...] = packed[index, 0 : ref.shape[0], :]


def shards(n_row, n_col, points, targets, probes, lengthscale, outputscale, noise):
    feats, width = points.shape
    n_probes = probes.shape[0]
    n_quad = n_col // 2
    rhs_rows = up_to(n_probes + 1, 8)
    lhs_rows = up_to(n_probes + 1, 16)
    rows = feats + rhs_rows
    group = 2 if n_quad % 2 == 0 else 1
    lanes = up_to(3 * rhs_rows, 128)
    vmem = pl.BlockSpec(memory_space=pltpu.VMEM)
    smem = pl.BlockSpec(memory_space=pltpu.SMEM)
    hbm = pl.BlockSpec(memory_space=pltpu.HBM)
    dma = pltpu.SemaphoreType.DMA
    packed = pl.pallas_call(
        functools.partial(kernel, n_row, n_col, feats, n_probes),
        out_shape=jax.ShapeDtypeStruct((5, rhs_rows, width), F32),
        in_specs=[hbm, hbm, hbm, smem, smem, smem],
        out_specs=vmem,
        scratch_shapes=[
            pltpu.VMEM((n_row, rows, width), F32),
            pltpu.VMEM((n_row, rows, width), F32),
            pltpu.VMEM((n_quad, feats, width), F32),
            pltpu.VMEM((1, width), F32),
            pltpu.VMEM((n_quad * width, 6 * feats), BF16),
            pltpu.VMEM((n_quad * width, 2 * width), F32),
            pltpu.VMEM((n_quad // group, lhs_rows, 2 * group * width), F32),
            pltpu.VMEM((n_quad, rhs_rows + n_probes, width), F32),
            pltpu.VMEM((n_quad, rhs_rows + n_probes, width), F32),
            pltpu.VMEM((n_row, 1, lanes), F32),
            pltpu.VMEM((n_col, 1, lanes), F32),
            dma((3,)),
            dma((n_row,)),
            dma((n_row,)),
            dma((n_row,)),
            dma((n_row,)),
            dma((n_quad,)),
            dma((n_quad,)),
            dma((n_quad,)),
            dma((n_quad,)),
            dma((n_row,)),
            dma((n_row,)),
            dma((n_col,)),
            dma((n_col,)),
        ],
        compiler_params=pltpu.CompilerParams(
            collective_id=0, has_side_effects=True, vmem_limit_bytes=60 << 20
        ),
    )(points, targets[None, :], probes, lengthscale, outputscale, noise)
    tall = jax.ShapeDtypeStruct((n_probes + 1, width), F32)
    short = jax.ShapeDtypeStruct((n_probes, width), F32)
    return pl.pallas_call(
        unpack,
        out_shape=(tall, tall, tall, short, short),
        in_specs=[vmem],
        out_specs=(vmem,) * 5,
    )(packed)


def solution(mesh):
    split = ("row", "col")
    wide = P(None, split)
    return jax.shard_map(
        functools.partial(shards, mesh.shape["row"], mesh.shape["col"]),
        mesh=mesh,
        in_specs=(wide, P(split), wide, P(), P(), P()),
        out_specs=(wide,) * 5,
        check_vma=False,
    )
```

time: 33.5 us -> 30 us (0.90)
  Pallas kernels: 30.7 us -> 27.2 us
    pallas_call x1, Pallas kernels: 3.68 us -> 1.53 us  [shards(): pl.pallas_call(unpack, out_shape=(tall, tall, tall, short, short), in_spe...]
    pallas_call x1, Pallas kernels: 27.1 us -> 25.7 us  [shards(): pl.pallas_call(functools.partial(kernel, n_row, n_col, feats, n_probes),...]
where the time goes in v3:
time: 30 us; the launch traced here: 29.8 us
  Pallas kernels  27.2 us (91%)
  between operations  2.58 us (9%)
    pallas_call x1, Pallas kernels, shards(): pl.pallas_call(functools.partial(kernel, n_row, n_col, feats, n_probes),...  25.7 us
    pallas_call x1, Pallas kernels, shards(): pl.pallas_call(unpack, out_shape=(tall, tall, tall, short, short), in_spe...  1.53 us

profile of v3, /device:TPU:0, one launch (start us, length us, event | category | flops | bytes accessed | tf_op | source)
XLA Modules:
  0.0 29.8 jit_solution(8710203478128921071)
XLA Ops:
  2.6 25.7 %shard_map.101.packed = f32[5,40,128]{2,1,0:T(8,128)} custom-call(f32[64,128]{1,0:T(8,128)} %x_hbm.1, f32[1,128]{1,0:T(1,128)} %bitcast.1, f32[32,128]{1,0:T(8,128)} %p_hbm.1, f32[1]{0:T(128)S(6)} %copy.11.ls_ref, f32[1]{0:T(128)S(6)} %copy.12.os_ref, f32[1]{0:T(128)S(6)} %copy.13.no_ref), custom_call_target="tpu_custom_call" | custom-call | tf_op jit(solution)/shard_map/pallas_call | solution.py:361
  28.2 1.5 %shard_map.102 = (f32[33,128]{1,0:T(8,128)}, f32[33,128]{1,0:T(8,128)}, f32[33,128]{1,0:T(8,128)}, f32[32,128]{1,0:T(8,128)}, f32[32,128]{1,0:T(8,128)}) custom-call(f32[5,40,128]{2,1,0:T(8,128)} %shard_map.101.packed), custom_call_target="tpu_custom_call" | custom-call | tf_op jit(solution)/shard_map/pallas_call | solution.py:398

commit v4 on v3

--- a/solution.py
+++ b/solution.py
@@ -54,8 +54,7 @@
     acc,
     part_out,
     part_in,
-    line_sums,
-    plane_sums,
+    sums,
     load_sem,
     line_send,
     line_recv,
@@ -65,10 +64,8 @@
     plane_recv,
     part_send,
     part_recv,
-    ls_send,
-    ls_recv,
-    ps_send,
-    ps_recv,
+    sum_send,
+    sum_recv,
 ):
     r = lax.axis_index("row")
     col = lax.axis_index("col")
@@ -90,10 +87,10 @@
     barrier = pltpu.get_barrier_semaphore()
 
     def on_line(k):
-        return (r + k) % n_row
+        return lax.rem(r + k, n_row)
 
     def on_plane(k):
-        return (col + k) % n_col
+        return lax.rem(col + k, n_col)
 
     def greet(row, column):
         pl.semaphore_signal(
@@ -273,43 +270,29 @@
         precision=lax.Precision.HIGHEST,
         preferred_element_type=F32,
     )
-    line_sums[r] = row_sums[0:1]
-
-    def line_share(k):
-        row = on_line(k)
-        return copy(line_sums.at[r], line_sums.at[r], ls_send.at[row], ls_recv.at[r], row, col)
-
-    def plane_share(k):
-        column = on_plane(k)
+    me = r * n_col + col
+    n_devices = n_row * n_col
+    sums[me] = row_sums[0:1]
+
+    def share(k):
+        peer = lax.rem(me + k, n_devices)
         return copy(
-            plane_sums.at[col], plane_sums.at[col], ps_send.at[column], ps_recv.at[col], r, column
-        )
-
-    each(1, n_row, lambda k: line_share(k).start())
+            sums.at[me], sums.at[me], sum_send.at[0], sum_recv.at[0],
+            lax.div(peer, n_col), lax.rem(peer, n_col),
+        )
+
+    @pl.loop(1, n_devices)
+    def _(k):
+        share(k).start()
 
     tall = n_probes + 1
     out_ref[3, 0:n_probes, :] = (scale / (ls_ref[0] * ls_ref[0] * ls_ref[0])) * ed
     out_ref[4, 0:n_probes, :] = eb[0:n_probes]
 
-    def line_arrived(k):
-        row = on_line(k)
-        slot = line_sums.at[row]
-        copy(slot, slot, ls_send.at[row], ls_recv.at[row], row, col).wait_recv()
-
-    each(1, n_row, line_arrived)
-
-    plane_sums[col] = jnp.sum(line_sums[...], axis=0)
-
-    each(1, n_col, lambda k: plane_share(k).start())
-
-    def plane_arrived(k):
-        column = on_plane(k)
-        slot = plane_sums.at[column]
-        copy(slot, slot, ps_send.at[column], ps_recv.at[column], r, column).wait_recv()
-
-    each(1, n_col, plane_arrived)
-
-    total = jnp.sum(plane_sums[...], axis=0)
+    shares = sums.at[pl.ds(0, n_devices - 1)]
+    all_shares = copy(shares, shares, sum_send.at[0], sum_recv.at[0], r, mate)
+    all_shares.wait_recv()
+    total = jnp.sum(sums[...], axis=0)
     lane = lax.broadcasted_iota(jnp.int32, (rhs_rows, lanes), 1)
     sub = lax.broadcasted_iota(jnp.int32, (rhs_rows, lanes), 0)
 
@@ -328,7 +311,6 @@
 
     def line_left(k):
         block_to(on_line(k)).wait_send()
-        line_share(k).wait_send()
 
     def quad_left(k):
         feats_to(chunk(k)).wait_send()
@@ -337,7 +319,7 @@
     each(1, n_row, line_left)
     each(0, n_row, lambda row: to_mate(row).wait_send())
     each(1, n_quad, quad_left)
-    each(1, n_col, lambda k: plane_share(k).wait_send())
+    all_shares.wait_send()
 
 
 def unpack(packed, sol_ref, res_ref, dir_ref, len_ref, scl_ref):
@@ -373,8 +355,7 @@
             pltpu.VMEM((n_quad // group, lhs_rows, 2 * group * width), F32),
             pltpu.VMEM((n_quad, rhs_rows + n_probes, width), F32),
             pltpu.VMEM((n_quad, rhs_rows + n_probes, width), F32),
-            pltpu.VMEM((n_row, 1, lanes), F32),
-            pltpu.VMEM((n_col, 1, lanes), F32),
+            pltpu.VMEM((n_row * n_col, 1, lanes), F32),
             dma((3,)),
             dma((n_row,)),
             dma((n_row,)),
@@ -384,10 +365,8 @@
             dma((n_quad,)),
             dma((n_quad,)),
             dma((n_quad,)),
-            dma((n_row,)),
-            dma((n_row,)),
-            dma((n_col,)),
-            dma((n_col,)),
+            dma((1,)),
+            dma((1,)),
         ],
         compiler_params=pltpu.CompilerParams(
             collective_id=0, has_side_effects=True, vmem_limit_bytes=60 << 20

time: 30 us -> 27.7 us (0.923)
  Pallas kernels: 27.2 us -> 24.9 us
    pallas_call x1, Pallas kernels: 25.7 us -> 23.4 us  [shards(): pl.pallas_call(functools.partial(kernel, n_row, n_col, feats, n_probes),...]
where the time goes in v4:
time: 27.7 us; the launch traced here: 27.5 us
  Pallas kernels  24.9 us (90%)
  between operations  2.58 us (9%)
    pallas_call x1, Pallas kernels, shards(): pl.pallas_call(functools.partial(kernel, n_row, n_col, feats, n_probes),...  23.4 us
    pallas_call x1, Pallas kernels, shards(): pl.pallas_call(unpack, out_shape=(tall, tall, tall, short, short), in_spe...  1.53 us

profile of v4, /device:TPU:0, one launch (start us, length us, event | category | flops | bytes accessed | tf_op | source)
XLA Modules:
  0.0 27.5 jit_solution(13410554987798554854)
XLA Ops:
  2.6 23.4 %shard_map.101.packed = f32[5,40,128]{2,1,0:T(8,128)} custom-call(f32[64,128]{1,0:T(8,128)} %x_hbm.1, f32[1,128]{1,0:T(1,128)} %bitcast.1, f32[32,128]{1,0:T(8,128)} %p_hbm.1, f32[1]{0:T(128)S(6)} %copy.11.ls_ref, f32[1]{0:T(128)S(6)} %copy.12.os_ref, f32[1]{0:T(128)S(6)} %copy.13.no_ref), custom_call_target="tpu_custom_call" | custom-call | tf_op jit(solution)/shard_map/pallas_call | solution.py:343
  26.0 1.5 %shard_map.102 = (f32[33,128]{1,0:T(8,128)}, f32[33,128]{1,0:T(8,128)}, f32[33,128]{1,0:T(8,128)}, f32[32,128]{1,0:T(8,128)}, f32[32,128]{1,0:T(8,128)}) custom-call(f32[5,40,128]{2,1,0:T(8,128)} %shard_map.101.packed), custom_call_target="tpu_custom_call" | custom-call | tf_op jit(solution)/shard_map/pallas_call | solution.py:377

commit v5 on v4

--- a/solution.py
+++ b/solution.py
@@ -26,7 +26,7 @@
 
 
 def each(first, last, use):
-    if last - first <= 7:
+    if last - first <= 8:
         for k in range(first, last):
             use(k)
     else:
@@ -169,19 +169,18 @@
     inv_two = 0.5 / (ls_ref[0] * ls_ref[0])
 
     def prepare(k):
-        x = jnp.transpose(plane[chunk(k)])
-        rows = pl.ds(pl.multiple_of(k * width, width), width)
-        own_sq[rows, :] = jnp.broadcast_to(
-            jnp.sum(x * x, axis=1, keepdims=True), (width, 2 * width)
-        )
-        high, middle, low = split_three(-2.0 * x)
-        own_split[rows, :] = jnp.concatenate([high, high, middle, high, low, middle], 1)
+        x = plane[chunk(k)]
+        lanes_k = pl.ds(pl.multiple_of(k * width, width), width)
+        own_sq[:, lanes_k] = jnp.sum(x * x, axis=0, keepdims=True)
+        high, middle, low = split_three(x)
+        own_split[:, lanes_k] = jnp.concatenate([high, middle, high, low, high, middle], 0)
 
     def open_pair(row):
         x = jnp.concatenate([held[row, 0:feats, :], other[row, 0:feats, :]], 1)
-        high, middle, low = split_three(x)
-        stack = jnp.concatenate([high, middle, high, low, high, middle], 0)
-        sq = jnp.sum(x * x, axis=0, keepdims=True)
+        x = jnp.transpose(x)
+        high, middle, low = split_three(-2.0 * x)
+        stack = jnp.concatenate([high, high, middle, high, low, middle], 1)
+        sq = jnp.sum(x * x, axis=1, keepdims=True)
         rhs = jnp.concatenate([held[row, feats:, :], other[row, feats:, :]], 1)
         rhs = jnp.concatenate([rhs, jnp.zeros((lhs_rows - rhs_rows, 2 * width), F32)], 0)
         b_high, b_middle, b_low = split_three(rhs)
@@ -197,15 +196,15 @@
 
     def absorb(opened, index):
         stack, sq, lhs_three, lhs_two = opened
-        rows = pl.ds(pl.multiple_of(index * span, span), span)
-        dots = jnp.dot(own_split[rows, :], stack, preferred_element_type=F32)
-        dist = jnp.maximum((own_sq[rows, :] + sq) + dots, 0.0)
+        own = pl.ds(pl.multiple_of(index * span, span), span)
+        dots = jnp.dot(stack, own_split[:, own], preferred_element_type=F32)
+        dist = jnp.maximum((sq + own_sq[:, own]) + dots, 0.0)
         kern = jnp.exp(dist * (-inv_two))
-        both = jnp.concatenate([kern, kern * dist], 0)
+        both = jnp.concatenate([kern, kern * dist], 1)
         both_high = both.astype(BF16)
         both_middle = (both - both_high.astype(F32)).astype(BF16)
-        first = lax.dot_general(lhs_three, both_high, NT, preferred_element_type=F32)
-        second = lax.dot_general(lhs_two, both_middle, NT, preferred_element_type=F32)
+        first = jnp.dot(lhs_three, both_high, preferred_element_type=F32)
+        second = jnp.dot(lhs_two, both_middle, preferred_element_type=F32)
         small = (first[2 * lhs_rows :] + second[lhs_rows:]) + (
             first[lhs_rows : 2 * lhs_rows] + second[:lhs_rows]
         )
@@ -229,6 +228,14 @@
 
     each(1, n_quad, prepare_other)
     n_groups = n_quad // group
+
+    def each_group(first, use):
+        if n_groups <= 2:
+            for index in range(first, n_groups):
+                use(index)
+        else:
+            pl.loop(first, n_groups)(use)
+
     for t in range(n_row):
         if t + 1 < n_row:
             block_from(order(t + 1)).wait_recv()
@@ -238,14 +245,14 @@
         copy(arrival, arrival, mate_send.at[row], mate_recv.at[row], r, mate).wait_recv()
         opened = open_pair(row)
         if t < n_row - 1:
-            each(0, n_groups, lambda index: absorb(opened, index))
+            each_group(0, lambda index: absorb(opened, index))
         else:
 
             def finish(index, own_too=False):
                 absorb(opened, index)
                 send_parts(index, own_too)
 
-            each(1, n_groups, finish)
+            each_group(1, finish)
             finish(0, True)
 
     part_in[q] = part_out[q]
@@ -274,16 +281,12 @@
     n_devices = n_row * n_col
     sums[me] = row_sums[0:1]
 
-    def share(k):
-        peer = lax.rem(me + k, n_devices)
-        return copy(
-            sums.at[me], sums.at[me], sum_send.at[0], sum_recv.at[0],
-            lax.div(peer, n_col), lax.rem(peer, n_col),
-        )
-
-    @pl.loop(1, n_devices)
-    def _(k):
-        share(k).start()
+    def share(row, column):
+        return copy(sums.at[me], sums.at[me], sum_send.at[0], sum_recv.at[0], row, column)
+
+    for dr in range(n_row):
+        row = on_line(dr)
+        each(1 if dr == 0 else 0, n_col, lambda k: share(row, on_plane(k)).start())
 
     tall = n_probes + 1
     out_ref[3, 0:n_probes, :] = (scale / (ls_ref[0] * ls_ref[0] * ls_ref[0])) * ed
@@ -350,8 +353,8 @@
             pltpu.VMEM((n_row, rows, width), F32),
             pltpu.VMEM((n_quad, feats, width), F32),
             pltpu.VMEM((1, width), F32),
-            pltpu.VMEM((n_quad * width, 6 * feats), BF16),
-            pltpu.VMEM((n_quad * width, 2 * width), F32),
+            pltpu.VMEM((6 * feats, n_quad * width), BF16),
+            pltpu.VMEM((1, n_quad * width), F32),
             pltpu.VMEM((n_quad // group, lhs_rows, 2 * group * width), F32),
             pltpu.VMEM((n_quad, rhs_rows + n_probes, width), F32),
             pltpu.VMEM((n_quad, rhs_rows + n_probes, width), F32),

time: 27.7 us -> 28.1 us (1.014)
  Pallas kernels: 24.9 us -> 25.3 us
    pallas_call x1, Pallas kernels: 23.4 us -> 23.7 us  [shards(): pl.pallas_call(functools.partial(kernel, n_row, n_col, feats, n_probes),...]
where the time goes in v5:
time: 28.1 us; the launch traced here: 27.8 us
  Pallas kernels  25.3 us (90%)
  between operations  2.58 us (9%)
    pallas_call x1, Pallas kernels, shards(): pl.pallas_call(functools.partial(kernel, n_row, n_col, feats, n_probes),...  23.7 us
    pallas_call x1, Pallas kernels, shards(): pl.pallas_call(unpack, out_shape=(tall, tall, tall, short, short), in_spe...  1.53 us

profile of v5, /device:TPU:0, one launch (start us, length us, event | category | flops | bytes accessed | tf_op | source)
XLA Modules:
  0.0 27.8 jit_solution(18362661983651122192)
XLA Ops:
  2.6 23.7 %shard_map.101.packed = f32[5,40,128]{2,1,0:T(8,128)} custom-call(f32[64,128]{1,0:T(8,128)} %x_hbm.1, f32[1,128]{1,0:T(1,128)} %bitcast.1, f32[32,128]{1,0:T(8,128)} %p_hbm.1, f32[1]{0:T(128)S(6)} %copy.11.ls_ref, f32[1]{0:T(128)S(6)} %copy.12.os_ref, f32[1]{0:T(128)S(6)} %copy.13.no_ref), custom_call_target="tpu_custom_call" | custom-call | tf_op jit(solution)/shard_map/pallas_call | solution.py:346
  26.3 1.5 %shard_map.102 = (f32[33,128]{1,0:T(8,128)}, f32[33,128]{1,0:T(8,128)}, f32[33,128]{1,0:T(8,128)}, f32[32,128]{1,0:T(8,128)}, f32[32,128]{1,0:T(8,128)}) custom-call(f32[5,40,128]{2,1,0:T(8,128)} %shard_map.101.packed), custom_call_target="tpu_custom_call" | custom-call | tf_op jit(solution)/shard_map/pallas_call | solution.py:380

commit v6 on v4

--- a/solution.py
+++ b/solution.py
@@ -81,9 +81,6 @@
         pltpu.make_async_copy(p_hbm, mine.at[feats : feats + n_probes], load_sem.at[1]),
         pltpu.make_async_copy(t_hbm, targets, load_sem.at[2]),
     ]
-    for load in loads:
-        load.start()
-
     barrier = pltpu.get_barrier_semaphore()
 
     def on_line(k):
@@ -98,6 +95,8 @@
         )
 
     each(1, n_row, lambda k: greet(on_line(k), col))
+    for load in loads:
+        load.start()
     each(1, n_col, lambda k: greet(r, on_plane(k)))
 
     acc[...] = jnp.zeros_like(acc)
@@ -161,10 +160,9 @@
         x, y = q % 2, q // 2
         return (q, y * 2 + 1 - x, (1 - y) * 2 + x, 3 - q)[k]
 
+    each(1, n_row, lambda t: block_to(order(n_row - t)).start())
     to_mate(r).start()
-    block_to(order(1)).start()
     each(1, n_quad, lambda k: feats_to(chunk(k)).start())
-    each(2, n_row, lambda t: block_to(order(t)).start())
     plane[q] = mine[0:feats, :]
     inv_two = 0.5 / (ls_ref[0] * ls_ref[0])
 

time: 27.7 us -> 27.8 us (level)
  no operation moved by 1% of the time
where the time goes in v6:
time: 27.8 us; the launch traced here: 27.6 us
  Pallas kernels  25 us (90%)
  between operations  2.58 us (9%)
    pallas_call x1, Pallas kernels, shards(): pl.pallas_call(functools.partial(kernel, n_row, n_col, feats, n_probes),...  23.5 us
    pallas_call x1, Pallas kernels, shards(): pl.pallas_call(unpack, out_shape=(tall, tall, tall, short, short), in_spe...  1.53 us

profile of v6, /device:TPU:0, one launch (start us, length us, event | category | flops | bytes accessed | tf_op | source)
XLA Modules:
  0.0 27.6 jit_solution(15458232812464070030)
XLA Ops:
  2.6 23.5 %shard_map.101.packed = f32[5,40,128]{2,1,0:T(8,128)} custom-call(f32[64,128]{1,0:T(8,128)} %x_hbm.1, f32[1,128]{1,0:T(1,128)} %bitcast.1, f32[32,128]{1,0:T(8,128)} %p_hbm.1, f32[1]{0:T(128)S(6)} %copy.11.ls_ref, f32[1]{0:T(128)S(6)} %copy.12.os_ref, f32[1]{0:T(128)S(6)} %copy.13.no_ref), custom_call_target="tpu_custom_call" | custom-call | tf_op jit(solution)/shard_map/pallas_call | solution.py:341
  26.1 1.5 %shard_map.102 = (f32[33,128]{1,0:T(8,128)}, f32[33,128]{1,0:T(8,128)}, f32[33,128]{1,0:T(8,128)}, f32[32,128]{1,0:T(8,128)}, f32[32,128]{1,0:T(8,128)}) custom-call(f32[5,40,128]{2,1,0:T(8,128)} %shard_map.101.packed), custom_call_target="tpu_custom_call" | custom-call | tf_op jit(solution)/shard_map/pallas_call | solution.py:375
